TPU v7x, 32 devices: a whole 2x2x4 slice. The times are simulated.
32 devices in a mesh: section: 2 (over x), dp: 16 (over z, y, core).
Axes of the slice: x: 2, y: 2, z: 4, core: 2. Of those that a mesh axis runs over, the one named last changes fastest.
Arguments:
- rows_in: bfloat16 [2, 192, 256, 384], P('section', 'dp'), may hold values from -6 to 6
- rows_cot: bfloat16 [2, 192, 256, 384], P('section', 'dp'), may hold values from -6 to 6
- counts: int32 [192], P('dp'), may hold values from 32 to 128, as said below
- codes: int32 [192, 128], P('dp'), may hold values from 0 to 4095
- codebook: float32 [4096, 12], replicated, may hold values from -6 to 6
- first_gain: float32 [2, 384], P('section'), may hold values from 0.5 to 1.5
- first_bias: float32 [2, 384], P('section'), may hold values from -1.75 to 1.75
- joint_weight: bfloat16 [2, 384, 1152], P('section'), may hold values from -0.3125 to 0.3125
- mixer_weight: bfloat16 [2, 384, 384], P('section'), may hold values from -2.5 to 2.5
- mixer_bias: float32 [2, 384], P('section'), may hold values from -1.75 to 1.75
- second_gain: float32 [2, 384], P('section'), may hold values from 0.5 to 1.5
- second_bias: float32 [2, 384], P('section'), may hold values from -1.75 to 1.75
- expand_weight: bfloat16 [2, 384, 1536], P('section'), may hold values from -0.3125 to 0.3125
- expand_bias: float32 [2, 1536], P('section'), may hold values from -3 to 3
- reduce_weight: bfloat16 [2, 1536, 384], P('section'), may hold values from -0.15625 to 0.15625
- reduce_bias: float32 [2, 384], P('section'), may hold values from -1.75 to 1.75
- latent_rows: float32 [2, 128, 384], P('section'), may hold values from -6 to 6
- latent_map: bfloat16 [2, 384, 12], P('section'), may hold values from -0.625 to 0.625
Outputs:
- rows_out: bfloat16 [2, 192, 256, 384], P('section', 'dp')
- rows_grad: float32 [2, 192, 256, 384], P('section', 'dp')
- first_gain_grad: float32 [2, 384], P('section')
- first_bias_grad: float32 [2, 384], P('section')
- joint_weight_grad: float32 [2, 384, 1152], P('section')
- mixer_weight_grad: float32 [2, 384, 384], P('section')
- mixer_bias_grad: float32 [2, 384], P('section')
- second_gain_grad: float32 [2, 384], P('section')
- second_bias_grad: float32 [2, 384], P('section')
- expand_weight_grad: float32 [2, 384, 1536], P('section')
- expand_bias_grad: float32 [2, 1536], P('section')
- reduce_weight_grad: float32 [2, 1536, 384], P('section')
- reduce_bias_grad: float32 [2, 384], P('section')
- latent_rows_grad: float32 [2, 128, 384], P('section')
- latent_map_grad: float32 [2, 384, 12], P('section')
Inputs may be any that keep to these rules, and one draw needn't show every extreme that they name: `counts`: each image's count is one quarter, one half or all of 128; its first count latents are live.
All inputs are finite; a program needn't handle non-finite values.
Results may differ from a plain program's by a relative error of at most 0.0099.
Values may be sent and summed in bfloat16 or wider, within the bound.
A program may use at most 192 MiB of HBM per device.

v0:
```python
from functools import partial

import jax
import jax.numpy as jnp
from jax import lax
from jax.sharding import PartitionSpec as P

HEADS = 6
HEAD_DIM = 64
MICRO = 6


commit_weight = 0.25
norm_eps = 1e-05
masked_score = -1e30


def passed_along(value, axis, steps):
    count = lax.axis_size(axis)
    first, last = (max(0, -steps), min(count, count - steps))
    return lax.ppermute(value, axis, [(source, source + steps) for source in range(first, last)])


def layer_norm(values, gain, offset):
    center = values - jnp.mean(values, -1, keepdims=True)
    spread = jnp.mean(center * center, -1, keepdims=True)
    return center * lax.rsqrt(spread + norm_eps) * gain + offset


def exact_gelu(values):
    return jax.nn.gelu(values, approximate=False)


def split_heads(joint, start):
    width = HEADS * HEAD_DIM
    return joint[:, :, start * width : (start + 1) * width].reshape(
        joint.shape[0], joint.shape[1], HEADS, HEAD_DIM
    )


def head_scores(query_rows, key_rows, live_keys):
    scores = jnp.einsum("nrhk,nchk->nhrc", query_rows, key_rows, preferred_element_type=jnp.float32)
    scores = scores * HEAD_DIM ** (-0.5)
    return jnp.where(live_keys[:, None, None, :], scores, masked_score)


def block_forward(params, stream, live_keys):
    (
        first_gain,
        first_bias,
        joint_weight,
        mixer_weight,
        mixer_bias,
        second_gain,
        second_bias,
        expand_weight,
        expand_bias,
        reduce_weight,
        reduce_bias,
    ) = params
    groups, rows = (stream.shape[0], stream.shape[1])
    normed = layer_norm(stream, first_gain, first_bias).astype(jnp.bfloat16)
    joint = jnp.einsum(
        "nrd,de->nre", normed, joint_weight, preferred_element_type=jnp.float32
    ).astype(jnp.bfloat16)
    scores = head_scores(split_heads(joint, 0), split_heads(joint, 1), live_keys)
    highest = jnp.max(scores, -1, keepdims=True)
    log_total = highest + jnp.log(jnp.sum(jnp.exp(scores - highest), -1, keepdims=True))
    probs = jnp.exp(scores - log_total).astype(jnp.bfloat16)
    mixed = jnp.einsum(
        "nhrc,nchk->nrhk", probs, split_heads(joint, 2), preferred_element_type=jnp.float32
    )
    mixed = mixed.reshape(groups, rows, HEADS * HEAD_DIM).astype(jnp.bfloat16)
    middle = (
        stream
        + jnp.einsum("nrd,de->nre", mixed, mixer_weight, preferred_element_type=jnp.float32)
        + mixer_bias
    )
    second = layer_norm(middle, second_gain, second_bias).astype(jnp.bfloat16)
    hidden = (
        jnp.einsum("nrd,df->nrf", second, expand_weight, preferred_element_type=jnp.float32)
        + expand_bias
    )
    active = exact_gelu(hidden).astype(jnp.bfloat16)
    output = (
        middle
        + jnp.einsum("nrf,fd->nrd", active, reduce_weight, preferred_element_type=jnp.float32)
        + reduce_bias
    )
    return (output, (stream, normed, joint, log_total, mixed, middle, second, hidden, active))


def block_backward(params, saved, grad_out, live_keys):
    (
        first_gain,
        first_bias,
        joint_weight,
        mixer_weight,
        mixer_bias,
        second_gain,
        second_bias,
        expand_weight,
        expand_bias,
        reduce_weight,
        reduce_bias,
    ) = params
    stream, normed, joint, log_total, mixed, middle, second, hidden, active = saved
    groups, rows = (stream.shape[0], stream.shape[1])
    grad_branch = grad_out.astype(jnp.bfloat16)
    reduce_grad = jnp.einsum("nrf,nrd->fd", active, grad_branch, preferred_element_type=jnp.float32)
    reduce_bias_grad = jnp.sum(grad_branch.astype(jnp.float32), (0, 1))
    grad_active = jnp.einsum(
        "nrd,fd->nrf", grad_branch, reduce_weight, preferred_element_type=jnp.float32
    )
    _, gelu_back = jax.vjp(exact_gelu, hidden)
    grad_hidden = gelu_back(grad_active)[0].astype(jnp.bfloat16)
    expand_grad = jnp.einsum("nrd,nrf->df", second, grad_hidden, preferred_element_type=jnp.float32)
    expand_bias_grad = jnp.sum(grad_hidden.astype(jnp.float32), (0, 1))
    grad_second = jnp.einsum(
        "nrf,df->nrd", grad_hidden, expand_weight, preferred_element_type=jnp.float32
    )
    _, second_back = jax.vjp(layer_norm, middle, second_gain, second_bias)
    grad_middle, second_gain_grad, second_bias_grad = second_back(grad_second)
    grad_middle = grad_middle + grad_out
    grad_mixer = grad_middle.astype(jnp.bfloat16)
    mixer_grad = jnp.einsum("nrd,nre->de", mixed, grad_mixer, preferred_element_type=jnp.float32)
    mixer_bias_grad = jnp.sum(grad_mixer.astype(jnp.float32), (0, 1))
    grad_mixed = jnp.einsum(
        "nre,de->nrd", grad_mixer, mixer_weight, preferred_element_type=jnp.float32
    )
    grad_mixed = grad_mixed.astype(jnp.bfloat16).reshape(groups, rows, HEADS, HEAD_DIM)
    query_rows = split_heads(joint, 0)
    key_rows = split_heads(joint, 1)
    value_rows = split_heads(joint, 2)
    probs = jnp.exp(head_scores(query_rows, key_rows, live_keys) - log_total)
    probs_low = probs.astype(jnp.bfloat16)
    grad_values = jnp.einsum(
        "nhrc,nrhk->nchk", probs_low, grad_mixed, preferred_element_type=jnp.float32
    )
    grad_probs = jnp.einsum(
        "nrhk,nchk->nhrc", grad_mixed, value_rows, preferred_element_type=jnp.float32
    )
    grad_scores = probs * (grad_probs - jnp.sum(probs * grad_probs, -1, keepdims=True))
    grad_scores = grad_scores.astype(jnp.bfloat16)
    scale = HEAD_DIM ** (-0.5)
    grad_queries = (
        jnp.einsum("nhrc,nchk->nrhk", grad_scores, key_rows, preferred_element_type=jnp.float32)
        * scale
    )
    grad_keys = (
        jnp.einsum("nhrc,nrhk->nchk", grad_scores, query_rows, preferred_element_type=jnp.float32)
        * scale
    )
    grad_joint = jnp.concatenate([grad_queries, grad_keys, grad_values], 2)
    grad_joint = grad_joint.reshape(groups, rows, 3 * HEADS * HEAD_DIM).astype(jnp.bfloat16)
    joint_grad = jnp.einsum("nrd,nre->de", normed, grad_joint, preferred_element_type=jnp.float32)
    grad_normed = jnp.einsum(
        "nre,de->nrd", grad_joint, joint_weight, preferred_element_type=jnp.float32
    )
    _, first_back = jax.vjp(layer_norm, stream, first_gain, first_bias)
    grad_stream, first_gain_grad, first_bias_grad = first_back(grad_normed)
    grad_stream = grad_stream + grad_middle
    return (
        grad_stream,
        (
            first_gain_grad,
            first_bias_grad,
            joint_grad,
            mixer_grad,
            mixer_bias_grad,
            second_gain_grad,
            second_bias_grad,
            expand_grad,
            expand_bias_grad,
            reduce_grad,
            reduce_bias_grad,
        ),
    )


def pick_block(stacked, index):
    return lax.dynamic_index_in_dim(stacked, index, 0, keepdims=False)


def per_device(
    rows_in,
    rows_cot,
    counts,
    codes,
    codebook,
    first_gain,
    first_bias,
    joint_weight,
    mixer_weight,
    mixer_bias,
    second_gain,
    second_bias,
    expand_weight,
    expand_bias,
    reduce_weight,
    reduce_bias,
    latent_rows,
    latent_map,
):
    params = (
        first_gain[0],
        first_bias[0],
        joint_weight[0],
        mixer_weight[0],
        mixer_bias[0],
        second_gain[0],
        second_bias[0],
        expand_weight[0],
        expand_bias[0],
        reduce_weight[0],
        reduce_bias[0],
    )
    lat_base = latent_rows[0]
    lat_map = latent_map[0]
    images, patch, width = (rows_in.shape[1], rows_in.shape[2], rows_in.shape[3])
    latents = latent_rows.shape[1]
    code_width = latent_map.shape[2]
    per_block = images // MICRO
    section_index = lax.axis_index("section")
    decoder_flag = section_index.astype(jnp.float32)
    quant = jnp.take(codebook, codes, axis=0)
    quant_low = quant.astype(jnp.bfloat16)
    live_lat = lax.broadcasted_iota(jnp.int32, (images, latents), 1) < counts[:, None]
    live_keys = jnp.concatenate([jnp.ones((images, patch), dtype=bool), live_lat], 1)
    embedded = jnp.einsum("nlc,dc->nld", quant_low, lat_map, preferred_element_type=jnp.float32)
    lat_input = lat_base[None] + embedded * decoder_flag

    def blocks(values):
        return values.reshape((MICRO, per_block) + values.shape[1:])

    rows_blocks = blocks(rows_in[0])
    cot_blocks = blocks(rows_cot[0])
    lat_blocks = blocks(lat_input)
    keys_blocks = blocks(live_keys)
    quant_blocks = blocks(quant)
    quant_low_blocks = blocks(quant_low)
    live_blocks = blocks(live_lat.astype(jnp.float32))

    def forward_step(carry, pieces):
        rows_part, lat_part, keys_part = pieces
        stream = jnp.concatenate([rows_part.astype(jnp.float32), lat_part], 1)
        output, saved = block_forward(params, stream, keys_part)
        lat_low = output[:, patch:].astype(jnp.bfloat16)
        latent_codes = jnp.einsum(
            "nld,dc->nlc", lat_low, lat_map, preferred_element_type=jnp.float32
        )
        received = passed_along(latent_codes.astype(jnp.bfloat16), "section", 1)
        return (carry, (output[:, :patch].astype(jnp.bfloat16), saved, lat_low, received))

    _, (out_blocks, saved_all, lat_low_all, received_all) = lax.scan(
        forward_step, jnp.zeros((), jnp.float32), (rows_blocks, lat_blocks, keys_blocks)
    )

    def backward_step(carry, step):
        grads, code_prev, rows_grad = carry
        index = step - 1 + section_index
        valid = ((index >= 0) & (index < MICRO)).astype(jnp.float32)
        chosen = jnp.clip(index, 0, MICRO - 1)
        take = partial(pick_block, index=chosen)
        saved = jax.tree.map(take, saved_all)
        keys_part = take(keys_blocks)
        cot_part = take(cot_blocks).astype(jnp.float32) * valid
        lat_cot = jnp.einsum("nlc,dc->nld", code_prev, lat_map, preferred_element_type=jnp.float32)
        grad_stream, block_grads = block_backward(
            params, saved, jnp.concatenate([cot_part, lat_cot], 1), keys_part
        )
        grad_lat = grad_stream[:, patch:]
        grad_embed = grad_lat.astype(jnp.bfloat16)
        map_project = jnp.einsum(
            "nld,nlc->dc", take(lat_low_all), code_prev, preferred_element_type=jnp.float32
        )
        map_embed = jnp.einsum(
            "nld,nlc->dc", grad_embed, take(quant_low_blocks), preferred_element_type=jnp.float32
        )
        grad_quant = jnp.einsum(
            "nld,dc->nlc", grad_embed, lat_map, preferred_element_type=jnp.float32
        )
        commit_term = (
            2.0
            * commit_weight
            * take(live_blocks)[:, :, None]
            * (take(received_all).astype(jnp.float32) - take(quant_blocks))
        )
        code_grad = ((grad_quant + commit_term * valid) * decoder_flag).astype(jnp.bfloat16)
        code_next = passed_along(code_grad, "section", -1)
        fresh = block_grads + (jnp.sum(grad_lat, 0), map_project + decoder_flag * map_embed)
        grads = jax.tree.map(jnp.add, grads, tuple(fresh))
        updated = (
            lax.dynamic_index_in_dim(rows_grad, chosen, 0, keepdims=False) + grad_stream[:, :patch]
        )
        rows_grad = lax.dynamic_update_index_in_dim(rows_grad, updated, chosen, 0)
        return ((grads, code_next, rows_grad), None)

    zero_grads = tuple((jnp.zeros(weight.shape, jnp.float32) for weight in params)) + (
        jnp.zeros((latents, width), jnp.float32),
        jnp.zeros((width, code_width), jnp.float32),
    )
    init = (
        zero_grads,
        jnp.zeros((per_block, latents, code_width), jnp.bfloat16),
        jnp.zeros((MICRO, per_block, patch, width), jnp.float32),
    )
    (grads, _, rows_grad), _ = lax.scan(backward_step, init, jnp.arange(MICRO + 1))
    grads = lax.psum(
        (
            grads[0],
            grads[1],
            grads[2],
            grads[3],
            grads[4],
            grads[5],
            grads[6],
            grads[7],
            grads[8],
            grads[9],
            grads[10],
            grads[11],
            grads[12],
        ),
        "dp",
    )
    rows_out = out_blocks.reshape(1, images, patch, width)
    rows_grad = rows_grad.reshape(1, images, patch, width)
    return (
        rows_out,
        rows_grad,
        grads[0][None],
        grads[1][None],
        grads[2][None],
        grads[3][None],
        grads[4][None],
        grads[5][None],
        grads[6][None],
        grads[7][None],
        grads[8][None],
        grads[9][None],
        grads[10][None],
        grads[11][None],
        grads[12][None],
    )


def solution(mesh):
    placed = (
        P("section", "dp", None, None),
        P("section", "dp", None, None),
        P("dp"),
        P("dp", None),
        P(),
        P("section", None),
        P("section", None),
        P("section", None, None),
        P("section", None, None),
        P("section", None),
        P("section", None),
        P("section", None),
        P("section", None, None),
        P("section", None),
        P("section", None, None),
        P("section", None),
        P("section", None, None),
        P("section", None, None),
    )
    return jax.shard_map(
        per_device,
        mesh=mesh,
        in_specs=placed,
        out_specs=(
            P("section", "dp", None, None),
            P("section", "dp", None, None),
            P("section", None),
            P("section", None),
            P("section", None, None),
            P("section", None, None),
            P("section", None),
            P("section", None),
            P("section", None),
            P("section", None, None),
            P("section", None),
            P("section", None, None),
            P("section", None),
            P("section", None, None),
            P("section", None, None),
        ),
        check_vma=False,
    )
```

profile of v0, /device:TPU:0, one launch (start us, length us, event | category | flops | bytes accessed | tf_op | source)
XLA Modules:
  0.0 1147.8 jit_solution(9476527106157732729)
XLA Ops:
  16.2 4.3 copy.73
  24.8 331.8 %while.73 = (s32[]{:T(128)}, bf16[6,2,256,384]{3,2,1,0:T(8,128)(2,1)}, f32[6,2,384,384]{2,3,1,0:T(8,128)}, bf16[6,2,384,384]{2,3,1,0:T(8,128)(2,1)}, bf16[6,2,38...) while((s32[]{:T(128)}, ...), condition=%wide.region_7.8_spmd, body=%wide.region_0.7_spmd.sunk | while | flops 3305865216 | bytes 111172440 | solution.py:255
  47.4 4.2 fusion.236
  51.7 11.9 %bitcast_dynamic-update-slice_fusion.18 = (bf16[6,2,384,1536]{3,2,1,0:T(8,128)(2,1)}, bf16[2,384,1536]{2,1,0:T(8,128)(2,1)S(1)}) fusion(bf16[6,2,384,1536]{3,2,1,0:T(8,128)(2,1)} %get-tuple-element.1773, s32[]{:T(128)S(6)} %copy.148, u8[384,1536]{1,0:T(8,128)(4,1)S(1)} %get-tuple-element.1644, u8[384,1536]{1,0:T(8,128)(4,1)S(1)} %get-tuple-element.1645, ...), kind=kLoop, calls=%fused_computation.174.clone.1 | loop fusion | flops 83755008 | bytes 10622980 | tf_op jit(solution)/shard_map/while/body/jit(dynamic_update_index_in_dim)/dynamic_update_slice | solution.py:255
  66.2 5.4 collective-permute-start
  105.6 4.2 fusion.236
  109.8 11.9 %bitcast_dynamic-update-slice_fusion.18 = (bf16[6,2,384,1536]{3,2,1,0:T(8,128)(2,1)}, bf16[2,384,1536]{2,1,0:T(8,128)(2,1)S(1)}) fusion(bf16[6,2,384,1536]{3,2,1,0:T(8,128)(2,1)} %get-tuple-element.1773, s32[]{:T(128)S(6)} %copy.148, u8[384,1536]{1,0:T(8,128)(4,1)S(1)} %get-tuple-element.1644, u8[384,1536]{1,0:T(8,128)(4,1)S(1)} %get-tuple-element.1645, ...), kind=kLoop, calls=%fused_computation.174.clone.1 | loop fusion | flops 83755008 | bytes 10622980 | tf_op jit(solution)/shard_map/while/body/jit(dynamic_update_index_in_dim)/dynamic_update_slice | solution.py:255
  160.3 4.2 fusion.236
  164.6 11.9 %bitcast_dynamic-update-slice_fusion.18 = (bf16[6,2,384,1536]{3,2,1,0:T(8,128)(2,1)}, bf16[2,384,1536]{2,1,0:T(8,128)(2,1)S(1)}) fusion(bf16[6,2,384,1536]{3,2,1,0:T(8,128)(2,1)} %get-tuple-element.1773, s32[]{:T(128)S(6)} %copy.148, u8[384,1536]{1,0:T(8,128)(4,1)S(1)} %get-tuple-element.1644, u8[384,1536]{1,0:T(8,128)(4,1)S(1)} %get-tuple-element.1645, ...), kind=kLoop, calls=%fused_computation.174.clone.1 | loop fusion | flops 83755008 | bytes 10622980 | tf_op jit(solution)/shard_map/while/body/jit(dynamic_update_index_in_dim)/dynamic_update_slice | solution.py:255
  215.0 4.2 fusion.236
  219.3 11.9 %bitcast_dynamic-update-slice_fusion.18 = (bf16[6,2,384,1536]{3,2,1,0:T(8,128)(2,1)}, bf16[2,384,1536]{2,1,0:T(8,128)(2,1)S(1)}) fusion(bf16[6,2,384,1536]{3,2,1,0:T(8,128)(2,1)} %get-tuple-element.1773, s32[]{:T(128)S(6)} %copy.148, u8[384,1536]{1,0:T(8,128)(4,1)S(1)} %get-tuple-element.1644, u8[384,1536]{1,0:T(8,128)(4,1)S(1)} %get-tuple-element.1645, ...), kind=kLoop, calls=%fused_computation.174.clone.1 | loop fusion | flops 83755008 | bytes 10622980 | tf_op jit(solution)/shard_map/while/body/jit(dynamic_update_index_in_dim)/dynamic_update_slice | solution.py:255
  269.6 4.2 fusion.236
  273.9 11.9 %bitcast_dynamic-update-slice_fusion.18 = (bf16[6,2,384,1536]{3,2,1,0:T(8,128)(2,1)}, bf16[2,384,1536]{2,1,0:T(8,128)(2,1)S(1)}) fusion(bf16[6,2,384,1536]{3,2,1,0:T(8,128)(2,1)} %get-tuple-element.1773, s32[]{:T(128)S(6)} %copy.148, u8[384,1536]{1,0:T(8,128)(4,1)S(1)} %get-tuple-element.1644, u8[384,1536]{1,0:T(8,128)(4,1)S(1)} %get-tuple-element.1645, ...), kind=kLoop, calls=%fused_computation.174.clone.1 | loop fusion | flops 83755008 | bytes 10622980 | tf_op jit(solution)/shard_map/while/body/jit(dynamic_update_index_in_dim)/dynamic_update_slice | solution.py:255
  324.4 4.2 fusion.236
  328.7 11.9 %bitcast_dynamic-update-slice_fusion.18 = (bf16[6,2,384,1536]{3,2,1,0:T(8,128)(2,1)}, bf16[2,384,1536]{2,1,0:T(8,128)(2,1)S(1)}) fusion(bf16[6,2,384,1536]{3,2,1,0:T(8,128)(2,1)} %get-tuple-element.1773, s32[]{:T(128)S(6)} %copy.148, u8[384,1536]{1,0:T(8,128)(4,1)S(1)} %get-tuple-element.1644, u8[384,1536]{1,0:T(8,128)(4,1)S(1)} %get-tuple-element.1645, ...), kind=kLoop, calls=%fused_computation.174.clone.1 | loop fusion | flops 83755008 | bytes 10622980 | tf_op jit(solution)/shard_map/while/body/jit(dynamic_update_index_in_dim)/dynamic_update_slice | solution.py:255
  359.7 611.3 %while.74 = (s32[]{:T(128)}, f32[384]{0:T(512)}, f32[384]{0:T(512)}, f32[384,1152]{1,0:T(8,128)}, f32[384,384]{1,0:T(8,128)}, /*index=5*/f32[384]{0:T(512)}, f32...) while((s32[]{:T(128)}, f32[384]{0:T(512)}, ...), condition=%wide.region_26.27_spmd.clone, body=%wide.region_8.26_spmd.clone.sunk | while | flops 6718880768 | bytes 271378144 | solution.py:308
  381.0 14.8 %convert_reduce_fusion.5 = (f32[1536]{0:T(1024)}, bf16[2,384,1536]{2,1,0:T(8,128)(2,1)S(1)}) fusion(bf16[1536,384]{1,0:T(8,128)(2,1)} %get-tuple-element.1944, f32[2,128,384]{2,1,0:T(8,128)S(1)} %fusion.268, f32[2,256,384]{2,1,0:T(8,128)S(1)} %multiply_bitcast_fusion.2, f32[6,2,384,1536]{3,2,1,0:T(8,128)} %get-tuple-element.1941, s32[]{:T(128)S(6)} %min.9), kind=kOutput, calls=%fused_computation.20.clone.1 | convolution fusion | flops 994441728 | bytes 9443332 | tf_op jit(solution)/shard_map/while/body/eval_jaxpr/nrd,fd->nrf/dot_general | solution.py:112
  449.7 4.2 fusion.282
  464.9 14.8 %convert_reduce_fusion.5 = (f32[1536]{0:T(1024)}, bf16[2,384,1536]{2,1,0:T(8,128)(2,1)S(1)}) fusion(bf16[1536,384]{1,0:T(8,128)(2,1)} %get-tuple-element.1944, f32[2,128,384]{2,1,0:T(8,128)S(1)} %fusion.268, f32[2,256,384]{2,1,0:T(8,128)S(1)} %multiply_bitcast_fusion.2, f32[6,2,384,1536]{3,2,1,0:T(8,128)} %get-tuple-element.1941, s32[]{:T(128)S(6)} %min.9), kind=kOutput, calls=%fused_computation.20.clone.1 | convolution fusion | flops 994441728 | bytes 9443332 | tf_op jit(solution)/shard_map/while/body/eval_jaxpr/nrd,fd->nrf/dot_general | solution.py:112
  534.6 4.2 fusion.282
  550.4 14.8 %convert_reduce_fusion.5 = (f32[1536]{0:T(1024)}, bf16[2,384,1536]{2,1,0:T(8,128)(2,1)S(1)}) fusion(bf16[1536,384]{1,0:T(8,128)(2,1)} %get-tuple-element.1944, f32[2,128,384]{2,1,0:T(8,128)S(1)} %fusion.268, f32[2,256,384]{2,1,0:T(8,128)S(1)} %multiply_bitcast_fusion.2, f32[6,2,384,1536]{3,2,1,0:T(8,128)} %get-tuple-element.1941, s32[]{:T(128)S(6)} %min.9), kind=kOutput, calls=%fused_computation.20.clone.1 | convolution fusion | flops 994441728 | bytes 9443332 | tf_op jit(solution)/shard_map/while/body/eval_jaxpr/nrd,fd->nrf/dot_general | solution.py:112
  620.1 4.2 fusion.282
  635.9 14.8 %convert_reduce_fusion.5 = (f32[1536]{0:T(1024)}, bf16[2,384,1536]{2,1,0:T(8,128)(2,1)S(1)}) fusion(bf16[1536,384]{1,0:T(8,128)(2,1)} %get-tuple-element.1944, f32[2,128,384]{2,1,0:T(8,128)S(1)} %fusion.268, f32[2,256,384]{2,1,0:T(8,128)S(1)} %multiply_bitcast_fusion.2, f32[6,2,384,1536]{3,2,1,0:T(8,128)} %get-tuple-element.1941, s32[]{:T(128)S(6)} %min.9), kind=kOutput, calls=%fused_computation.20.clone.1 | convolution fusion | flops 994441728 | bytes 9443332 | tf_op jit(solution)/shard_map/while/body/eval_jaxpr/nrd,fd->nrf/dot_general | solution.py:112
  705.6 4.2 fusion.282
  721.4 14.8 %convert_reduce_fusion.5 = (f32[1536]{0:T(1024)}, bf16[2,384,1536]{2,1,0:T(8,128)(2,1)S(1)}) fusion(bf16[1536,384]{1,0:T(8,128)(2,1)} %get-tuple-element.1944, f32[2,128,384]{2,1,0:T(8,128)S(1)} %fusion.268, f32[2,256,384]{2,1,0:T(8,128)S(1)} %multiply_bitcast_fusion.2, f32[6,2,384,1536]{3,2,1,0:T(8,128)} %get-tuple-element.1941, s32[]{:T(128)S(6)} %min.9), kind=kOutput, calls=%fused_computation.20.clone.1 | convolution fusion | flops 994441728 | bytes 9443332 | tf_op jit(solution)/shard_map/while/body/eval_jaxpr/nrd,fd->nrf/dot_general | solution.py:112
  791.1 4.2 fusion.282
  806.9 14.8 %convert_reduce_fusion.5 = (f32[1536]{0:T(1024)}, bf16[2,384,1536]{2,1,0:T(8,128)(2,1)S(1)}) fusion(bf16[1536,384]{1,0:T(8,128)(2,1)} %get-tuple-element.1944, f32[2,128,384]{2,1,0:T(8,128)S(1)} %fusion.268, f32[2,256,384]{2,1,0:T(8,128)S(1)} %multiply_bitcast_fusion.2, f32[6,2,384,1536]{3,2,1,0:T(8,128)} %get-tuple-element.1941, s32[]{:T(128)S(6)} %min.9), kind=kOutput, calls=%fused_computation.20.clone.1 | convolution fusion | flops 994441728 | bytes 9443332 | tf_op jit(solution)/shard_map/while/body/eval_jaxpr/nrd,fd->nrf/dot_general | solution.py:112
  876.6 4.2 fusion.282
  892.4 14.8 %convert_reduce_fusion.5 = (f32[1536]{0:T(1024)}, bf16[2,384,1536]{2,1,0:T(8,128)(2,1)S(1)}) fusion(bf16[1536,384]{1,0:T(8,128)(2,1)} %get-tuple-element.1944, f32[2,128,384]{2,1,0:T(8,128)S(1)} %fusion.268, f32[2,256,384]{2,1,0:T(8,128)S(1)} %multiply_bitcast_fusion.2, f32[6,2,384,1536]{3,2,1,0:T(8,128)} %get-tuple-element.1941, s32[]{:T(128)S(6)} %min.9), kind=kOutput, calls=%fused_computation.20.clone.1 | convolution fusion | flops 994441728 | bytes 9443332 | tf_op jit(solution)/shard_map/while/body/eval_jaxpr/nrd,fd->nrf/dot_general | solution.py:112
  962.1 4.2 fusion.282
  973.3 64.6 %all-reduce.1 = (f32[1,384]{1,0:T(1,128)}, f32[1,384]{1,0:T(1,128)}, f32[1,384]{1,0:T(1,128)}, f32[1,384]{1,0:T(1,128)}, f32[1,384]{1,0:T(1,128)}, /*index=5*/f3...) all-reduce(f32[1,384]{1,0:T(1,128)S(1)} %broadcast_in_dim.246, ...), channel_id=1, replica_groups=mesh['section'=2,'dp'=16] {'dp'}, use_global_device_ids=true, to_apply=%region_27.28 | all-reduce | flops 8448 | bytes 67584 | tf_op jit(solution)/shard_map/psum | solution.py:309
  1037.8 95.5 %all-reduce.5.cloned.1.call-done = (f32[1,384,1152]{2,1,0:T(8,128)}, f32[1,384,384]{2,1,0:T(8,128)}, f32[1,384,1536]{2,1,0:T(8,128)}, f32[1,1536,384]{2,1,0:T(8,128)}, f32[1,128,384]{2,1,0:T(8,128)}) async-done(((f32[1,384,1152]{2,1,0:T(8,128)}, f32[1,384,384]{2,1,0:T(8,128)}, f32[1,384,1536]{2,1,0:T(8,128)}, f32[1,1536,384]{2,1,0:T(8,128)}, f32[1,128,384]{2,1,0:T(8,128)}), (f32[1,384,1152]{2,1,0:T(8,128)}, ...) | async-done | bytes 7274512 | tf_op jit(solution)/shard_map/psum | solution.py:309
  (1622 shorter events, 708.8 us)
Async XLA Ops:
  7.2 1126.1 %all-reduce.5.cloned.1.call-start = ((), (), s32[]{:S(2)}) async-start(), calls=%async_computation | async-start | bytes 14548992 | tf_op jit(solution)/shard_map/psum | solution.py:309
  24.8 20.3 %copy-start.24 = (bf16[384,384]{0,1:T(8,128)(2,1)}, bf16[384,384]{0,1:T(8,128)(2,1)S(1)}, u32[]{:S(2)}) copy-start(bf16[384,384]{0,1:T(8,128)(2,1)S(1)} %get-tuple-element.1812) | copy-start | bytes 884740 | tf_op jit(solution)/shard_map/while
  66.2 15.5 %collective-permute-start = (bf16[2,128,12]{1,2,0:T(8,128)(2,1)}, bf16[2,128,12]{1,2,0:T(8,128)(2,1)}, u32[]{:S(2)}, u32[]{:S(2)}) collective-permute-start(bf16[2,128,12]{1,2,0:T(8,128)(2,1)} %convolution_convert_fusion.5), channel_id=1, source_target_pairs={{0,16},{1,17},{2,18},{3,19},{4,20},{5,21},{6,22},{7,23},{8,24},{9,... | collective-permute-start | bytes 18440 | tf_op jit(solution)/shard_map/while/body/eval_jaxpr/ppermute | solution.py:21
  83.0 20.3 %copy-start.24 = (bf16[384,384]{0,1:T(8,128)(2,1)}, bf16[384,384]{0,1:T(8,128)(2,1)S(1)}, u32[]{:S(2)}) copy-start(bf16[384,384]{0,1:T(8,128)(2,1)S(1)} %get-tuple-element.1812) | copy-start | bytes 884740 | tf_op jit(solution)/shard_map/while
  124.4 12.0 %collective-permute-start = (bf16[2,128,12]{1,2,0:T(8,128)(2,1)}, bf16[2,128,12]{1,2,0:T(8,128)(2,1)}, u32[]{:S(2)}, u32[]{:S(2)}) collective-permute-start(bf16[2,128,12]{1,2,0:T(8,128)(2,1)} %convolution_convert_fusion.5), channel_id=1, source_target_pairs={{0,16},{1,17},{2,18},{3,19},{4,20},{5,21},{6,22},{7,23},{8,24},{9,... | collective-permute-start | bytes 18440 | tf_op jit(solution)/shard_map/while/body/eval_jaxpr/ppermute | solution.py:21
  137.7 20.3 %copy-start.24 = (bf16[384,384]{0,1:T(8,128)(2,1)}, bf16[384,384]{0,1:T(8,128)(2,1)S(1)}, u32[]{:S(2)}) copy-start(bf16[384,384]{0,1:T(8,128)(2,1)S(1)} %get-tuple-element.1812) | copy-start | bytes 884740 | tf_op jit(solution)/shard_map/while
  179.1 12.0 %collective-permute-start = (bf16[2,128,12]{1,2,0:T(8,128)(2,1)}, bf16[2,128,12]{1,2,0:T(8,128)(2,1)}, u32[]{:S(2)}, u32[]{:S(2)}) collective-permute-start(bf16[2,128,12]{1,2,0:T(8,128)(2,1)} %convolution_convert_fusion.5), channel_id=1, source_target_pairs={{0,16},{1,17},{2,18},{3,19},{4,20},{5,21},{6,22},{7,23},{8,24},{9,... | collective-permute-start | bytes 18440 | tf_op jit(solution)/shard_map/while/body/eval_jaxpr/ppermute | solution.py:21
  233.8 12.0 %collective-permute-start = (bf16[2,128,12]{1,2,0:T(8,128)(2,1)}, bf16[2,128,12]{1,2,0:T(8,128)(2,1)}, u32[]{:S(2)}, u32[]{:S(2)}) collective-permute-start(bf16[2,128,12]{1,2,0:T(8,128)(2,1)} %convolution_convert_fusion.5), channel_id=1, source_target_pairs={{0,16},{1,17},{2,18},{3,19},{4,20},{5,21},{6,22},{7,23},{8,24},{9,... | collective-permute-start | bytes 18440 | tf_op jit(solution)/shard_map/while/body/eval_jaxpr/ppermute | solution.py:21
  288.5 12.1 %collective-permute-start = (bf16[2,128,12]{1,2,0:T(8,128)(2,1)}, bf16[2,128,12]{1,2,0:T(8,128)(2,1)}, u32[]{:S(2)}, u32[]{:S(2)}) collective-permute-start(bf16[2,128,12]{1,2,0:T(8,128)(2,1)} %convolution_convert_fusion.5), channel_id=1, source_target_pairs={{0,16},{1,17},{2,18},{3,19},{4,20},{5,21},{6,22},{7,23},{8,24},{9,... | collective-permute-start | bytes 18440 | tf_op jit(solution)/shard_map/while/body/eval_jaxpr/ppermute | solution.py:21
  301.9 20.3 %copy-start.24 = (bf16[384,384]{0,1:T(8,128)(2,1)}, bf16[384,384]{0,1:T(8,128)(2,1)S(1)}, u32[]{:S(2)}) copy-start(bf16[384,384]{0,1:T(8,128)(2,1)S(1)} %get-tuple-element.1812) | copy-start | bytes 884740 | tf_op jit(solution)/shard_map/while
  343.2 12.0 %collective-permute-start = (bf16[2,128,12]{1,2,0:T(8,128)(2,1)}, bf16[2,128,12]{1,2,0:T(8,128)(2,1)}, u32[]{:S(2)}, u32[]{:S(2)}) collective-permute-start(bf16[2,128,12]{1,2,0:T(8,128)(2,1)} %convolution_convert_fusion.5), channel_id=1, source_target_pairs={{0,16},{1,17},{2,18},{3,19},{4,20},{5,21},{6,22},{7,23},{8,24},{9,... | collective-permute-start | bytes 18440 | tf_op jit(solution)/shard_map/while/body/eval_jaxpr/ppermute | solution.py:21
  379.2 29.7 %copy-start.2 = (f32[2,256,384]{2,1,0:T(8,128)}, f32[2,256,384]{2,1,0:T(8,128)S(1)}, u32[]{:S(2)}) copy-start(f32[2,256,384]{2,1,0:T(8,128)S(1)} %multiply_bitcast_fusion.2) | copy-start | bytes 2359300 | tf_op jit(solution)/shard_map/while
  380.2 28.7 %copy-start.9 = (f32[2,128,384]{2,1,0:T(8,128)}, f32[2,128,384]{2,1,0:T(8,128)S(1)}, u32[]{:S(2)}) copy-start(f32[2,128,384]{2,1,0:T(8,128)S(1)} %fusion.268) | copy-start | bytes 1179652 | tf_op jit(solution)/shard_map/while
  435.2 22.2 %collective-permute-start.1 = (bf16[2,128,12]{1,2,0:T(8,128)(2,1)}, bf16[2,128,12]{1,2,0:T(8,128)(2,1)}, u32[]{:S(2)}, u32[]{:S(2)}) collective-permute-start(bf16[2,128,12]{1,2,0:T(8,128)(2,1)} %fusion.285), channel_id=1, source_target_pairs={{16,0},{17,1},{18,2},{19,3},{20,4},{21,5},{22,6},{23,7},{24,8},{25... | collective-permute-start | bytes 18440 | tf_op jit(solution)/shard_map/while/body/eval_jaxpr/ppermute | solution.py:21
  463.1 29.7 %copy-start.2 = (f32[2,256,384]{2,1,0:T(8,128)}, f32[2,256,384]{2,1,0:T(8,128)S(1)}, u32[]{:S(2)}) copy-start(f32[2,256,384]{2,1,0:T(8,128)S(1)} %multiply_bitcast_fusion.2) | copy-start | bytes 2359300 | tf_op jit(solution)/shard_map/while
  464.1 28.7 %copy-start.9 = (f32[2,128,384]{2,1,0:T(8,128)}, f32[2,128,384]{2,1,0:T(8,128)S(1)}, u32[]{:S(2)}) copy-start(f32[2,128,384]{2,1,0:T(8,128)S(1)} %fusion.268) | copy-start | bytes 1179652 | tf_op jit(solution)/shard_map/while
  519.1 23.8 %collective-permute-start.1 = (bf16[2,128,12]{1,2,0:T(8,128)(2,1)}, bf16[2,128,12]{1,2,0:T(8,128)(2,1)}, u32[]{:S(2)}, u32[]{:S(2)}) collective-permute-start(bf16[2,128,12]{1,2,0:T(8,128)(2,1)} %fusion.285), channel_id=1, source_target_pairs={{16,0},{17,1},{18,2},{19,3},{20,4},{21,5},{22,6},{23,7},{24,8},{25... | collective-permute-start | bytes 18440 | tf_op jit(solution)/shard_map/while/body/eval_jaxpr/ppermute | solution.py:21
  548.6 29.7 %copy-start.2 = (f32[2,256,384]{2,1,0:T(8,128)}, f32[2,256,384]{2,1,0:T(8,128)S(1)}, u32[]{:S(2)}) copy-start(f32[2,256,384]{2,1,0:T(8,128)S(1)} %multiply_bitcast_fusion.2) | copy-start | bytes 2359300 | tf_op jit(solution)/shard_map/while
  549.6 28.7 %copy-start.9 = (f32[2,128,384]{2,1,0:T(8,128)}, f32[2,128,384]{2,1,0:T(8,128)S(1)}, u32[]{:S(2)}) copy-start(f32[2,128,384]{2,1,0:T(8,128)S(1)} %fusion.268) | copy-start | bytes 1179652 | tf_op jit(solution)/shard_map/while
  604.6 23.8 %collective-permute-start.1 = (bf16[2,128,12]{1,2,0:T(8,128)(2,1)}, bf16[2,128,12]{1,2,0:T(8,128)(2,1)}, u32[]{:S(2)}, u32[]{:S(2)}) collective-permute-start(bf16[2,128,12]{1,2,0:T(8,128)(2,1)} %fusion.285), channel_id=1, source_target_pairs={{16,0},{17,1},{18,2},{19,3},{20,4},{21,5},{22,6},{23,7},{24,8},{25... | collective-permute-start | bytes 18440 | tf_op jit(solution)/shard_map/while/body/eval_jaxpr/ppermute | solution.py:21
  634.1 29.7 %copy-start.2 = (f32[2,256,384]{2,1,0:T(8,128)}, f32[2,256,384]{2,1,0:T(8,128)S(1)}, u32[]{:S(2)}) copy-start(f32[2,256,384]{2,1,0:T(8,128)S(1)} %multiply_bitcast_fusion.2) | copy-start | bytes 2359300 | tf_op jit(solution)/shard_map/while
  635.1 28.7 %copy-start.9 = (f32[2,128,384]{2,1,0:T(8,128)}, f32[2,128,384]{2,1,0:T(8,128)S(1)}, u32[]{:S(2)}) copy-start(f32[2,128,384]{2,1,0:T(8,128)S(1)} %fusion.268) | copy-start | bytes 1179652 | tf_op jit(solution)/shard_map/while
  690.1 23.8 %collective-permute-start.1 = (bf16[2,128,12]{1,2,0:T(8,128)(2,1)}, bf16[2,128,12]{1,2,0:T(8,128)(2,1)}, u32[]{:S(2)}, u32[]{:S(2)}) collective-permute-start(bf16[2,128,12]{1,2,0:T(8,128)(2,1)} %fusion.285), channel_id=1, source_target_pairs={{16,0},{17,1},{18,2},{19,3},{20,4},{21,5},{22,6},{23,7},{24,8},{25... | collective-permute-start | bytes 18440 | tf_op jit(solution)/shard_map/while/body/eval_jaxpr/ppermute | solution.py:21
  719.6 29.7 %copy-start.2 = (f32[2,256,384]{2,1,0:T(8,128)}, f32[2,256,384]{2,1,0:T(8,128)S(1)}, u32[]{:S(2)}) copy-start(f32[2,256,384]{2,1,0:T(8,128)S(1)} %multiply_bitcast_fusion.2) | copy-start | bytes 2359300 | tf_op jit(solution)/shard_map/while
  720.6 28.7 %copy-start.9 = (f32[2,128,384]{2,1,0:T(8,128)}, f32[2,128,384]{2,1,0:T(8,128)S(1)}, u32[]{:S(2)}) copy-start(f32[2,128,384]{2,1,0:T(8,128)S(1)} %fusion.268) | copy-start | bytes 1179652 | tf_op jit(solution)/shard_map/while
  775.6 23.8 %collective-permute-start.1 = (bf16[2,128,12]{1,2,0:T(8,128)(2,1)}, bf16[2,128,12]{1,2,0:T(8,128)(2,1)}, u32[]{:S(2)}, u32[]{:S(2)}) collective-permute-start(bf16[2,128,12]{1,2,0:T(8,128)(2,1)} %fusion.285), channel_id=1, source_target_pairs={{16,0},{17,1},{18,2},{19,3},{20,4},{21,5},{22,6},{23,7},{24,8},{25... | collective-permute-start | bytes 18440 | tf_op jit(solution)/shard_map/while/body/eval_jaxpr/ppermute | solution.py:21
  805.1 29.7 %copy-start.2 = (f32[2,256,384]{2,1,0:T(8,128)}, f32[2,256,384]{2,1,0:T(8,128)S(1)}, u32[]{:S(2)}) copy-start(f32[2,256,384]{2,1,0:T(8,128)S(1)} %multiply_bitcast_fusion.2) | copy-start | bytes 2359300 | tf_op jit(solution)/shard_map/while
  806.1 28.7 %copy-start.9 = (f32[2,128,384]{2,1,0:T(8,128)}, f32[2,128,384]{2,1,0:T(8,128)S(1)}, u32[]{:S(2)}) copy-start(f32[2,128,384]{2,1,0:T(8,128)S(1)} %fusion.268) | copy-start | bytes 1179652 | tf_op jit(solution)/shard_map/while
  861.1 23.8 %collective-permute-start.1 = (bf16[2,128,12]{1,2,0:T(8,128)(2,1)}, bf16[2,128,12]{1,2,0:T(8,128)(2,1)}, u32[]{:S(2)}, u32[]{:S(2)}) collective-permute-start(bf16[2,128,12]{1,2,0:T(8,128)(2,1)} %fusion.285), channel_id=1, source_target_pairs={{16,0},{17,1},{18,2},{19,3},{20,4},{21,5},{22,6},{23,7},{24,8},{25... | collective-permute-start | bytes 18440 | tf_op jit(solution)/shard_map/while/body/eval_jaxpr/ppermute | solution.py:21
  890.6 29.7 %copy-start.2 = (f32[2,256,384]{2,1,0:T(8,128)}, f32[2,256,384]{2,1,0:T(8,128)S(1)}, u32[]{:S(2)}) copy-start(f32[2,256,384]{2,1,0:T(8,128)S(1)} %multiply_bitcast_fusion.2) | copy-start | bytes 2359300 | tf_op jit(solution)/shard_map/while
  891.6 28.7 %copy-start.9 = (f32[2,128,384]{2,1,0:T(8,128)}, f32[2,128,384]{2,1,0:T(8,128)S(1)}, u32[]{:S(2)}) copy-start(f32[2,128,384]{2,1,0:T(8,128)S(1)} %fusion.268) | copy-start | bytes 1179652 | tf_op jit(solution)/shard_map/while
  946.6 23.8 %collective-permute-start.1 = (bf16[2,128,12]{1,2,0:T(8,128)(2,1)}, bf16[2,128,12]{1,2,0:T(8,128)(2,1)}, u32[]{:S(2)}, u32[]{:S(2)}) collective-permute-start(bf16[2,128,12]{1,2,0:T(8,128)(2,1)} %fusion.285), channel_id=1, source_target_pairs={{16,0},{17,1},{18,2},{19,3},{20,4},{21,5},{22,6},{23,7},{24,8},{25... | collective-permute-start | bytes 18440 | tf_op jit(solution)/shard_map/while/body/eval_jaxpr/ppermute | solution.py:21
  (452 other events, 2047.5 us)
Sparse Core Ops, SparseCore 0:
  971.3 161.9 all-reduce.4
where the time goes:
time: 1170 us; the launch traced here: 1150 us
  matrix products  407 us (35%)
  other arithmetic  298 us (25%)
  local copies, waits for them, and re-layouts  219 us (19%)
  waiting for transfers between devices  95.5 us (8%)
  blocking collectives  64.6 us (6%)
  loops' own time  25 us (2%)
  starting transfers between devices  23.8 us (2%)
  between operations  14.7 us (1%)
    dynamic_update_slice x30, other arithmetic, per_device(): lax.scan(forward_step, jnp.zeros((), jnp.float32), (rows_blocks, lat_bloc...  109 us
    dot_general x7, matrix products, block_backward(): jnp.einsum('nrd,fd->nrf', grad_branch, reduce_weight, preferred_element_t...  104 us
    psum x1, waiting for transfers between devices, per_device(): lax.psum((grads[0], grads[1], grads[2], grads[3], grads[4], grads[5], gra...  95.5 us
    psum x1, blocking collectives, per_device(): lax.psum((grads[0], grads[1], grads[2], grads[3], grads[4], grads[5], gra...  64.6 us
    dynamic_slice x28, local copies, waits for them, and re-layouts, pick_block(): return lax.dynamic_index_in_dim(stacked, index, 0, keepdims=False)  52 us
    slice x31, local copies, waits for them, and re-layouts, split_heads(): joint[:, :, start * width:(start + 1) * width]  41.5 us
    reduce_sum x34, other arithmetic, layer_norm(): center = values - jnp.mean(values, -1, keepdims=True)  40.6 us
    dynamic_update_slice x30, local copies, waits for them, and re-layouts, per_device(): lax.scan(forward_step, jnp.zeros((), jnp.float32), (rows_blocks, lat_bloc...  33.3 us
  transfers between devices with their start and end apart: 14, of which 1 were waited for; matrix products, arithmetic and copies ran while one was open for 17% of the time, Pallas kernels for 0%

commit v1 on v0

v1 whole, which is shorter than its diff:
```python
import functools

import jax
import jax.numpy as jnp
from jax import lax
from jax.experimental import pallas as pl
from jax.experimental.pallas import tpu as pltpu
from jax.sharding import PartitionSpec as P

HEADS = 6
PAIRS = 3
LANES = 128
CODE_ROWS = 16
GROUP = 256
commit_weight = 0.25
norm_eps = 1e-05
masked_score = -1e30
LOG2E = 1.4426950408889634
MESH = pl.DeviceIdType.MESH
f32 = jnp.float32
bf16 = jnp.bfloat16
VMEM_BYTES = 63 * 1024 * 1024


def dot_nn(a, b):
    return lax.dot_general(a, b, (((1,), (0,)), ((), ())), preferred_element_type=f32)


def dot_nt(a, b):
    return lax.dot_general(a, b, (((1,), (1,)), ((), ())), preferred_element_type=f32)


def dot_tn(a, b):
    return lax.dot_general(a, b, (((0,), (0,)), ((), ())), preferred_element_type=f32)


def stacked_halves(values):
    lane = lax.broadcasted_iota(jnp.int32, (1, LANES), 1)
    low = (lane < LANES // 2).astype(f32)
    return jnp.concatenate([values * low.astype(bf16), values * (1.0 - low).astype(bf16)], 0)


def normalised(values):
    center = values - jnp.mean(values, -1, keepdims=True)
    spread = jnp.mean(center * center, -1, keepdims=True)
    factor = lax.rsqrt(spread + norm_eps)
    return center * factor, factor


def low(value):
    return jnp.asarray(value, bf16)


def gelu_pair(hidden):
    hidden = hidden.astype(bf16)
    square = hidden * hidden
    poly = low(3.63928092e-02) + square * (low(-8.82193757e-05) + square * (low(-3.66000625e-05) + square * low(1.41853336e-06)))
    phi = low(0.5) + low(0.5) * jnp.tanh(hidden * (low(7.97869556e-01) + square * poly))
    bell = jnp.exp2(square * low(-0.5 * LOG2E))
    return hidden * phi, phi + (hidden * low(0.3989422804014327)) * bell


def forward_body(
    is_encoder, image, counts_ref, rows_ref, codes_ref, base_ref, map_ref, book_ref,
    gain1_ref, bias1_ref, wj_ref, wm_ref, biasm_ref, gain2_ref, bias2_ref, we_ref, biase_ref, wr_ref, biasr_ref,
    out_ref, joint_ref, e_ref, rl_ref, mixed_ref, x1_ref, rs_ref, x2_ref, act_ref, dg_ref, latlow_ref, small_ref,
    map_rows, book_parts, quants,
):
    patch, width = rows_ref.shape[2], rows_ref.shape[3]
    rows = joint_ref.shape[1]
    latents = rows - patch
    ff = act_ref.shape[2]
    used = rows if is_encoder else patch
    if is_encoder:
        lat = base_ref[...]
    else:
        @pl.when(lax.rem(image, 2) == 0)
        def _():
            code = jnp.concatenate([codes_ref[pl.ds(image, 1), :], codes_ref[pl.ds(image + 1, 1), :]], 1)
            entry = lax.broadcasted_iota(jnp.int32, (GROUP, 2 * latents), 0)
            within = jnp.where(entry == lax.rem(code, GROUP), 1.0, 0.0).astype(bf16)
            found = dot_nn(book_parts[...], within)
            tall = 3 * CODE_ROWS
            total = jnp.zeros((tall, 2 * latents), f32)
            for group in range(found.shape[0] // tall):
                here = jnp.where(lax.div(code, GROUP) == group, 1.0, 0.0)
                total = total + found[group * tall : (group + 1) * tall] * here
            quants[...] = total[:CODE_ROWS] + total[CODE_ROWS : 2 * CODE_ROWS] + total[2 * CODE_ROWS :]

        quant = jnp.where(lax.rem(image, 2) == 0, quants[:, :latents], quants[:, latents:])
        small_ref[0] = quant
        lat = base_ref[...] + dot_tn(quant.astype(bf16), map_rows[...])
    stream = jnp.concatenate([rows_ref[0, 0].astype(f32), lat], 0)
    xhat, factor1 = normalised(stream)
    x1_ref[0] = xhat.astype(bf16)
    normed = (xhat * gain1_ref[...] + bias1_ref[...]).astype(bf16)
    joint_ref[0] = dot_nn(normed, wj_ref[0]).astype(bf16)
    scale = (width // HEADS) ** -0.5 * LOG2E
    live = lax.broadcasted_iota(jnp.int32, (1, latents), 1) < counts_ref[image]
    mask = jnp.where(live, 0.0, masked_score)
    sums = stacked_halves(jnp.ones((rows, LANES), bf16))
    for pair in range(PAIRS):
        at = pair * LANES
        q = joint_ref[0, :used, at : at + LANES]
        k = joint_ref[0, :, width + at : width + at + LANES]
        v = joint_ref[0, :, 2 * width + at : 2 * width + at + LANES]
        scores = dot_nt(q, stacked_halves(k))
        shares = []
        for half in range(2):
            start = half * rows
            head = scores[:, start : start + patch]
            tail = scores[:, start + patch : start + rows] + mask
            top = jnp.maximum(jnp.max(head, -1, keepdims=True), jnp.max(tail, -1, keepdims=True))
            share = jnp.exp2((jnp.concatenate([head, tail], 1) - top) * scale).astype(bf16)
            e_ref[0, 2 * pair + half, :used] = share
            shares.append(share)
        gathered = dot_nn(jnp.concatenate(shares, 1), jnp.concatenate([stacked_halves(v), sums], 1))
        norm = 1.0 / gathered[:, LANES:]
        rl_ref[0, :used, at : at + LANES] = norm.astype(bf16)
        mixed_ref[0, :used, at : at + LANES] = (gathered[:, :LANES] * norm).astype(bf16)
    middle = stream[:used] + dot_nn(mixed_ref[0, :used], wm_ref[0]) + biasm_ref[...]
    xhat2, factor2 = normalised(middle)
    x2_ref[0, :used] = xhat2.astype(bf16)
    lane = lax.broadcasted_iota(jnp.int32, (used, LANES), 1)
    rs_ref[0, :used] = jnp.where(lane < LANES // 2, factor1[:used], factor2)
    second = (xhat2 * gain2_ref[...] + bias2_ref[...]).astype(bf16)
    cut = 256
    for at in range(0, ff, cut):
        hidden = dot_nn(second, we_ref[0, :, at : at + cut]) + biase_ref[:, at : at + cut]
        active, slope = gelu_pair(hidden)
        act_ref[0, :used, at : at + cut] = active.astype(bf16)
        dg_ref[0, :used, at : at + cut] = slope.astype(bf16)
    output = middle + dot_nn(act_ref[0, :used], wr_ref[0]) + biasr_ref[...]
    out_ref[0, 0] = output[:patch].astype(bf16)
    if is_encoder:
        low = output[patch:].astype(bf16)
        latlow_ref[0] = low
        small_ref[0] = dot_nt(map_rows[...], low)
    else:
        rs_ref[0, used:] = jnp.broadcast_to(factor1[used:], (latents, LANES))


def put_map_rows(map_ref, map_rows):
    map_rows[...] = jnp.zeros_like(map_rows)
    map_rows[: map_ref.shape[0]] = map_ref[...].astype(f32).astype(bf16)


def forward_kernel(*refs):
    image = pl.program_id(0)
    section = lax.axis_index("section")
    map_ref, book_ref, map_rows, book_parts = refs[4], refs[5], refs[-3], refs[-2]

    @pl.when(image == 0)
    def _():
        put_map_rows(map_ref, map_rows)

    @pl.when((image == 0) & (section == 1))
    def _():
        book_parts[...] = jnp.zeros_like(book_parts)
        left = book_ref[...]
        for index in range(3):
            low = left.astype(bf16)
            for group in range(book_ref.shape[1] // GROUP):
                start = (3 * group + index) * CODE_ROWS
                book_parts[start : start + book_ref.shape[0]] = low[:, group * GROUP : (group + 1) * GROUP]
            left = left - low.astype(f32)

    @pl.when(section == 0)
    def _():
        forward_body(True, image, *refs)

    @pl.when(section == 1)
    def _():
        forward_body(False, image, *refs)


def column_sum(values):
    return jnp.sum(values, 0, keepdims=True)


def norm_back(grad, xhat, factor, gain):
    scaled = grad * gain
    along = jnp.mean(scaled * xhat, -1, keepdims=True)
    return factor * (scaled - jnp.mean(scaled, -1, keepdims=True) - xhat * along)


def reach(devices):
    pair = 2 if devices % 2 == 0 else 1
    side = 2 if devices % (2 * pair) == 0 else 1
    line = 4 if devices % (4 * pair * side) == 0 else 1
    return pair, side, line, devices // (pair * side * line)


class Place:
    def __init__(self, sizes):
        self.pair, self.side, self.line, self.blocks = sizes
        me = lax.axis_index("dp")
        self.core = lax.rem(me, self.pair)
        self.flank = lax.rem(me // self.pair, self.side)
        self.spot = lax.rem(me // (self.pair * self.side), self.line)
        self.block = me // (self.pair * self.side * self.line)

    def at(self, core=None, flank=None, spot=None, block=None):
        core = self.core if core is None else core
        flank = self.flank if flank is None else flank
        spot = self.spot if spot is None else spot
        block = self.block if block is None else block
        return {"dp": ((block * self.line + spot) * self.side + flank) * self.pair + core}

    def other_core(self):
        return self.at(core=1 - self.core)

    def other_flank(self):
        return self.at(flank=1 - self.flank)

    def next_spot(self, step):
        return self.at(spot=lax.rem(self.spot + step, self.line))

    def next_block(self, step):
        return self.at(block=lax.rem(self.block + step, self.blocks))

    def others(self):
        found = [self.other_core()] if self.pair > 1 else []
        found += [self.other_flank()] if self.side > 1 else []
        found += [self.next_spot(step) for step in range(1, self.line)]
        return found + [self.next_block(step) for step in range(1, self.blocks)]


class Flow:
    def __init__(self, place, order, own, recv1, recv2, recv3, far3, final, result, send_sem, recv_sem):
        self.result = result
        self.place, self.order, self.own, self.final = place, order, own, final
        self.recv1, self.recv2, self.recv3, self.far3 = recv1, recv2, recv3, far3
        self.send_sem, self.recv_sem = send_sem, recv_sem
        self.dtype = own.dtype
        self.span = own.shape[1] // place.pair
        self.sides = own.shape[0] // place.side
        self.lines = self.sides // place.line
        self.stages = [0, 1, 2, 3, 5, 6, 7] if place.blocks == 1 else [0, 1, 2, 3, 4, 5, 6, 7]

    def copy(self, number, source, target, device):
        return pltpu.make_async_remote_copy(
            src_ref=source, dst_ref=target, send_sem=self.send_sem.at[self.order, number],
            recv_sem=self.recv_sem.at[self.order, number], device_id=device, device_id_type=MESH,
        )

    def cols(self, which):
        return pl.ds(pl.multiple_of(which * self.span, LANES), self.span)

    def side_rows(self, which):
        return pl.ds(pl.multiple_of(which * self.sides, 16), self.sides)

    def line_rows(self, which):
        return pl.ds(pl.multiple_of(which * self.lines, 16), self.lines)

    def final_rows(self):
        return pl.ds(pl.multiple_of(self.place.flank * self.sides + self.place.spot * self.lines, 16), self.lines)

    def deliver(self):
        return pltpu.make_async_copy(self.final, self.result, self.send_sem.at[self.order, 0])

    def sends(self, stage):
        place = self.place
        mine = self.cols(place.core)
        if stage == 0 and place.pair > 1:
            return [self.copy(0, self.own.at[:, self.cols(1 - place.core)], self.recv1, place.other_core())]
        if stage == 1 and place.side > 1:
            return [self.copy(1, self.recv1.at[self.side_rows(1 - place.flank)], self.recv2, place.other_flank())]
        if stage == 2:
            return [
                self.copy(
                    1 + step, self.recv2.at[self.line_rows(lax.rem(place.spot + step, place.line))], self.recv3.at[step - 1],
                    place.next_spot(step),
                )
                for step in range(1, place.line)
            ]
        if stage == 3:
            spot = self.far3.at[place.block]
            return [self.copy(4 + step, spot, spot, place.next_block(step)) for step in range(1, place.blocks)]
        if stage == 4:
            region = self.final.at[self.final_rows(), mine]
            return [self.copy(10 + step, region, region, place.next_spot(step)) for step in range(1, place.line)]
        if stage == 5 and place.side > 1:
            region = self.final.at[self.side_rows(place.flank), mine]
            return [self.copy(8, region, region, place.other_flank())]
        if stage == 6 and place.pair > 1:
            region = self.final.at[:, mine]
            return [self.copy(9, region, region, place.other_core())]
        return []

    def settle(self, stage):
        place = self.place
        mine = self.cols(place.core)
        for copy in self.sends(stage):
            copy.wait_recv()
        if stage == 0:
            total = self.own[:, mine].astype(f32)
            if place.pair > 1:
                total = total + self.recv1[...].astype(f32)
            self.recv1[...] = total.astype(self.dtype)
        elif stage == 1:
            total = self.recv1[self.side_rows(place.flank)].astype(f32)
            if place.side > 1:
                total = total + self.recv2[...].astype(f32)
            self.recv2[...] = total.astype(self.dtype)
        elif stage == 2:
            total = self.recv2[self.line_rows(place.spot)].astype(f32)
            for step in range(1, place.line):
                total = total + self.recv3[step - 1].astype(f32)
            if place.blocks > 1:
                self.far3[place.block] = total.astype(self.dtype)
            else:
                self.final[self.final_rows(), mine] = total.astype(self.dtype)
        elif stage == 3 and place.blocks > 1:
            total = self.far3[0].astype(f32)
            for index in range(1, place.blocks):
                total = total + self.far3[index].astype(f32)
            self.final[self.final_rows(), mine] = total.astype(self.dtype)

    def advance(self, turn):
        stage = self.stages[turn]
        if stage > 0:
            self.settle(stage - 1)
        if stage == 3 and self.place.blocks == 1:
            stage = 4
        for copy in self.sends(stage):
            copy.start()
        if stage == 7:
            for copy in self.sends(0):
                copy.wait_send()
            self.deliver().start()

    def drain(self):
        for stage in range(1, 7):
            if stage != 3 or self.place.blocks > 1:
                for copy in self.sends(stage):
                    copy.wait_send()
        self.deliver().wait()


LINK, CORE_LINK, LATENCY, POINT, TURN = 100e3, 300e3, 0.8, 0.95, 0.7


def planned(early, late, points, blocks):
    busy, state = {}, {}

    def enter(names, time):
        for name, size in names:
            uses = [("core", size / 2 / CORE_LINK), ("side", size / 2 / LINK), ("line", size / 2 / LINK)]
            if blocks > 1:
                uses.append(("far", size / 4 / LINK))
            state[name] = [0, time, uses + uses[2::-1]]

    def left(name):
        return state[name][0] <= len(state[name][2])

    def turn(name, time):
        entry = state[name]
        if entry[0] < len(entry[2]):
            link, span = entry[2][entry[0]]
            busy[link] = max(busy.get(link, 0.0), time) + span
            entry[1] = busy[link] + LATENCY
        entry[0] += 1
        return entry[0] - 1, time + TURN

    table, rest, time = [], [], 0.0
    enter(early, time)
    for _ in range(points):
        row = []
        for name in state:
            if left(name) and state[name][1] <= time:
                number, time = turn(name, time)
                row.append((name, number))
        table.append(row)
        time += POINT
    enter(late, time)
    while any(left(name) for name in state):
        name = min((state[name][1], name) for name in state if left(name))[1]
        number, time = turn(name, max(time, state[name][1]))
        rest.append((name, number))
    return table, rest


FIRST_GAIN, FIRST_BIAS, MIXER_BIAS, SECOND_GAIN, SECOND_BIAS, REDUCE_BIAS, EXPAND_BIAS, LATENT_MAP = 0, 1, 2, 3, 4, 5, 6, 16


def add_row(vectors, row, values):
    vectors[row : row + 1] += column_sum(values)


def branch_back(
    is_encoder, first, counts_ref, cot_ref, act_ref, latlow_ref, small_ref,
    acc_r, vectors, branch_keep, left_t, map_rows, code_in, code_copy,
):
    count, patch, width = cot_ref.shape[1:]
    rows = act_ref.shape[1]
    latents = rows - patch
    ff = act_ref.shape[2]
    used = rows if is_encoder else patch
    tall = count * used
    cot = cot_ref[0]
    if is_encoder:
        branches = []
        for index in range(count):
            image = first + index
            code_copy(image).wait_recv()
            live = lax.broadcasted_iota(jnp.int32, (1, latents), 1) < counts_ref[image]
            weight = jnp.where(live, 2.0 * commit_weight, 0.0)
            codes = (code_in[image] + weight * small_ref[index].astype(bf16).astype(f32)).astype(bf16)
            vectors[LATENT_MAP : LATENT_MAP + CODE_ROWS] += dot_nn(codes, latlow_ref[index])
            lat_cot = dot_tn(codes, map_rows[...])
            branches += [cot[index], lat_cot.astype(bf16)]
        branch = jnp.concatenate(branches, 0)
    else:
        branch = cot.reshape(tall, width)
    add_row(vectors, REDUCE_BIAS, branch.astype(f32))
    branch_keep[:tall] = branch
    left_t[0, :, :tall] = branch.T
    cut = 512
    for at in range(0, ff, cut):
        span = slice(at, at + cut)
        acc_r[:, span] += dot_nn(left_t[0, :, :tall], act_ref[:, :used, span].reshape(tall, cut))


def feed_forward_back(
    is_encoder, first, dg_ref, x2_ref, rs_ref, gain2_ref, bias2_ref, wm_ref, we_ref, wr_ref,
    vectors, hidden_sums, gmid_keep, pull_keep, ghid, branch_keep, left_t,
):
    count, rows, width = x2_ref.shape
    ff = dg_ref.shape[2]
    used = rows if is_encoder else rows * 2 // 3
    tall = count * used
    branch = branch_keep[:tall]
    grad_out = branch.astype(f32)
    xhat2 = x2_ref[:, :used].reshape(tall, width).astype(f32)
    second = (xhat2 * gain2_ref[...] + bias2_ref[...]).astype(bf16)
    left_t[1, :, :tall] = second.T
    cut = 512
    for at in range(0, ff, cut):
        span = slice(at, at + cut)
        grad_active = dot_nt(branch, wr_ref[0, span, :])
        grad_hidden = grad_active * dg_ref[:, :used, span].reshape(tall, cut).astype(f32)
        hidden_sums[:, span] += column_sum(grad_hidden)
        ghid[:tall, span] = grad_hidden.astype(bf16)
    grad_second = dot_nt(ghid[:tall], we_ref[0])
    add_row(vectors, SECOND_BIAS, grad_second)
    add_row(vectors, SECOND_GAIN, grad_second * xhat2)
    factor2 = rs_ref[:, :used, LANES // 2 : LANES // 2 + 1].reshape(tall, 1)
    grad_middle = norm_back(grad_second, xhat2, factor2, gain2_ref[...]) + grad_out
    grad_mixer = grad_middle.astype(bf16)
    add_row(vectors, MIXER_BIAS, grad_mixer.astype(f32))
    pulled = dot_nt(grad_mixer, wm_ref[0]).astype(bf16)
    ring = gmid_keep.shape[0]
    for index in range(count):
        spot = lax.rem(first + index, ring)
        span = slice(index * used, (index + 1) * used)
        gmid_keep[spot, :used] = grad_mixer[span]
        pull_keep[spot, :used] = pulled[span]


def feed_forward_gradients(is_encoder, first, mixed_ref, acc_e, acc_m, gmid_keep, ghid, left_t):
    count, rows = mixed_ref.shape[:2]
    ff = acc_e.shape[1]
    used = rows if is_encoder else rows * 2 // 3
    tall = count * used
    width = acc_m.shape[0]
    cut = 512
    for at in range(0, ff, cut):
        span = slice(at, at + cut)
        acc_e[:, span] += dot_nn(left_t[1, :, :tall], ghid[:tall, span])
    ring = gmid_keep.shape[0]
    grad_mixer = jnp.concatenate([gmid_keep[lax.rem(first + index, ring), :used] for index in range(count)], 0)
    acc_m[...] += dot_tn(mixed_ref[:, :used].reshape(tall, width), grad_mixer)


def attention_back(is_encoder, image, pairs, joint_ref, e_ref, rl_ref, mixed_ref, pull_keep, gjoints):
    rows, width = mixed_ref.shape[1:]
    gjoint = gjoints.at[lax.rem(image, 2)]
    used = rows if is_encoder else joint_patch(gjoint)
    spot = lax.rem(image, pull_keep.shape[0])
    scale = (width // HEADS) ** -0.5
    half = LANES // 2
    lane = lax.broadcasted_iota(jnp.int32, (used, LANES), 1)

    def own_parts(left, rights):
        made = dot_nn(left.T, jnp.concatenate(rights, 1))
        return jnp.concatenate([made[:half, :rows], made[half:, rows:]], 0)

    for pair in pairs:
        at = pair * LANES
        q = joint_ref[0, :used, at : at + LANES]
        k = joint_ref[0, :, width + at : width + at + LANES]
        v = joint_ref[0, :, 2 * width + at : 2 * width + at + LANES]
        pulled = pull_keep[spot, :used, at : at + LANES].astype(f32)
        pulled = pulled * (rl_ref[0, :used, at : at + LANES].astype(f32) * scale)
        pulled_low = pulled.astype(bf16)
        matched = pulled * mixed_ref[0, :used, at : at + LANES].astype(f32)
        matched_first = jnp.where(lane < half, matched, 0.0)
        shifts = (jnp.sum(matched_first, -1, keepdims=True), jnp.sum(matched - matched_first, -1, keepdims=True))
        grad_probs = dot_nt(pulled_low, stacked_halves(v))
        shares, grads = [], []
        for index in range(2):
            share = e_ref[0, 2 * pair + index, :used]
            shares.append(share)
            grads.append(share * (grad_probs[:, index * rows : (index + 1) * rows] - shifts[index]).astype(bf16))
        gjoint[:used, at : at + LANES] = dot_nn(jnp.concatenate(grads, 1), stacked_halves(k)).astype(bf16)
        gjoint[:, width + at : width + at + LANES] = own_parts(q, grads).astype(bf16).T
        gjoint[:, 2 * width + at : 2 * width + at + LANES] = (own_parts(pulled_low, shares) * (1.0 / scale)).astype(bf16).T
    if not is_encoder:
        gjoint[used:, :width] = jnp.zeros((rows - used, width), bf16)


def joint_patch(gjoint):
    return gjoint.shape[0] * 2 // 3


def first_norm_back(
    is_encoder, image, counts_ref, x1_ref, rs_ref, small_ref, gain1_ref, bias1_ref, wj_ref,
    acc_j, vectors, latent_sums, gmid_keep, gjoints, normed_t, rows_buf, map_rows, code_out, rows_wait,
):
    gjoint = gjoints.at[lax.rem(image, 2)]
    rows, width = x1_ref.shape[1:]
    patch = rows_buf.shape[1]
    latents = rows - patch
    used = rows if is_encoder else patch
    spot = lax.rem(image, gmid_keep.shape[0])
    xhat1 = x1_ref[0].astype(f32)
    normed = (xhat1 * gain1_ref[...] + bias1_ref[...]).astype(bf16)
    grad_normed = dot_nt(gjoint[...], wj_ref[0])
    if is_encoder:
        acc_j[...] += dot_nn(normed.T, gjoint[...])
    else:
        normed_t[lax.rem(image, 2)] = normed.T
    add_row(vectors, FIRST_BIAS, grad_normed)
    add_row(vectors, FIRST_GAIN, grad_normed * xhat1)
    grad_stream = norm_back(grad_normed, xhat1, rs_ref[0, :, 0:1], gain1_ref[...])
    grad_middle = gmid_keep[spot, :used].astype(f32)
    rows_wait(image)
    rows_buf[lax.rem(image, rows_buf.shape[0])] = (grad_stream[:patch] + grad_middle[:patch]).astype(bf16)
    grad_lat = grad_stream[patch:]
    if is_encoder:
        grad_lat = grad_lat + grad_middle[patch:]
    else:
        embed = grad_lat.astype(bf16)
        quant = small_ref[0]
        vectors[LATENT_MAP : LATENT_MAP + CODE_ROWS] += dot_nn(quant.astype(bf16), embed)
        live = lax.broadcasted_iota(jnp.int32, (1, latents), 1) < counts_ref[image]
        weight = jnp.where(live, 2.0 * commit_weight, 0.0)
        code_out[image] = dot_nt(map_rows[...], embed) - weight * quant
    latent_sums[...] += grad_lat


def ahead(images):
    return images // 2 - 1


def put_columns(targets, start, blocks):
    edges = [0]
    for target in targets:
        edges.append(edges[-1] + target.shape[1])
    for block in blocks:
        stop = start + block.shape[1]
        for target, low, high in zip(targets, edges[:-1], edges[1:]):
            left, right = max(low, start), min(high, stop)
            if left < right:
                target[:, left - low : right - low] = block[:, left - start : right - start]
        start = stop


def columns(sources, start, stop):
    found, low = [], 0
    for source in sources:
        high = low + source.shape[1]
        left, right = max(low, start), min(high, stop)
        if left < right:
            found.append(source[:, left - low : right - low])
        low = high
    return found[0] if len(found) == 1 else jnp.concatenate(found, 1)


def backward_kernel(
    sizes, counts_ref,
    cot_ref, act_ref, dg_ref, x2_ref, rs2_ref, mixed2_ref, latlow_ref, small2_ref,
    joint_a, e_a, rl_a, x1_a, mixed_a, rs_a, small_a, joint_b, e_b, rl_b, x1_b,
    map_ref, gain1_ref, bias1_ref, wj_ref, wm_ref, gain2_ref, bias2_ref, we_ref, wr_ref,
    rows_out, out_0, out_1, out_2, out_3,
    acc_r, acc_e, acc_j, acc_m, vectors, hidden_sums, latent_sums, gmid_keep, pull_keep, ghid, branch_keep, left_t, gjoints, normed_t, rows_buf, map_rows,
    code_in, code_out, code_send, code_recv, rows_sem, send_sem, recv_sem, *buffers,
):
    step = pl.program_id(0)
    steps = pl.num_programs(0)
    images = code_in.shape[0]
    half, early_images = images // 2, ahead(images)
    slots = rows_buf.shape[0]
    width = acc_m.shape[0]
    outs = (out_0, out_1, out_2, out_3)
    section = lax.axis_index("section")
    encoder, decoder = section == 0, section == 1
    partner = {"section": 1 - section}
    place = Place(sizes)
    others = place.others()
    barrier = pltpu.get_barrier_semaphore()

    def code_copy(index):
        return pltpu.make_async_remote_copy(
            src_ref=code_out.at[index], dst_ref=code_in.at[index], send_sem=code_send.at[index],
            recv_sem=code_recv.at[index], device_id=partner, device_id_type=MESH,
        )

    def rows_copy(index):
        return pltpu.make_async_copy(rows_buf.at[lax.rem(index, slots)], rows_out.at[0, index], rows_sem.at[index])

    def rows_wait(image):
        @pl.when(image >= slots)
        def _():
            rows_copy(image - slots).wait()

    @pl.when(step == 0)
    def _():
        for device in [partner] + others:
            pl.semaphore_signal(barrier, inc=1, device_id=device, device_id_type=MESH)
        put_map_rows(map_ref, map_rows)
        for ref in (acc_r, acc_e, acc_j, acc_m, vectors, hidden_sums, latent_sums):
            ref[...] = jnp.zeros_like(ref)

    branch_args = (counts_ref, cot_ref, act_ref, latlow_ref, small2_ref)
    branch_args += (acc_r, vectors, branch_keep, left_t, map_rows, code_in, code_copy)
    first_args = (dg_ref, x2_ref, rs2_ref, gain2_ref, bias2_ref, wm_ref, we_ref, wr_ref)
    first_args += (vectors, hidden_sums, gmid_keep, pull_keep, ghid, branch_keep, left_t)
    weight_args = (mixed2_ref, acc_e, acc_m, gmid_keep, ghid, left_t)
    norm_args = (gain1_ref, bias1_ref, wj_ref)
    norm_args += (acc_j, vectors, latent_sums, gmid_keep, gjoints, normed_t, rows_buf, map_rows, code_out, rows_wait)
    set_a = (joint_a, e_a, rl_a, mixed_a), (x1_a, rs_a, small_a)
    pair = [[ref.at[pl.ds(index, 1)] for ref in (mixed2_ref, rs2_ref, small2_ref)] for index in range(2)]
    pair_a = (joint_a, e_a, rl_a, pair[0][0]), (x1_a, pair[0][1], pair[0][2])
    pair_b = (joint_b, e_b, rl_b, pair[1][0]), (x1_b, pair[1][1], pair[1][2])

    def attention(is_encoder, image, refs, pairs=range(PAIRS)):
        attention_back(is_encoder, image, pairs, *refs[0], pull_keep, gjoints)

    def norm(is_encoder, image, refs):
        first_norm_back(is_encoder, image, counts_ref, *refs[1], *norm_args)
        rows_copy(image).start()

    def joint_gradient():
        left = jnp.concatenate([normed_t[0], normed_t[1]], 1)
        acc_j[...] += dot_nn(left, gjoints[...].reshape(2 * gjoints.shape[1], gjoints.shape[2]))

    image = early_images + step - half

    @pl.when(encoder & (step < half) & (image >= 0))
    def _():
        attention(True, image, set_a)
        norm(True, image, set_a)

    kinds = len(outs)
    early_names, late_names = (0, 1), (2, 3)
    flows = [Flow(place, kind, *buffers[6 * kind : 6 * kind + 6], outs[kind], send_sem, recv_sem) for kind in range(kinds)]
    own_early, own_late = [flow.own for flow in flows[:2]], [flow.own for flow in flows[2:]]

    def sizes_of(names):
        return [(name, flows[name].own.shape[0] * flows[name].own.shape[1] * flows[name].dtype.itemsize) for name in names]

    later_steps = images - early_images
    table, rest = planned(sizes_of(early_names), sizes_of(late_names), (PAIRS + 1) * later_steps, place.blocks)

    @pl.when(encoder & (step < half))
    def _():
        branch_back(True, 2 * step, *branch_args)

    def start_reduce():
        put_columns(own_early[:1], 0, [acc_r[:, at : at + width].astype(bf16).T for at in range(0, acc_r.shape[1], width)])
        flows[0].advance(0)

    @pl.when(encoder & (step == half - 1))
    def _():
        pl.semaphore_wait(barrier, 1 + len(others))
        start_reduce()

    @pl.when(encoder & (step < half))
    def _():
        feed_forward_back(True, 2 * step, *first_args)
        feed_forward_gradients(True, 2 * step, *weight_args)

    @pl.when(decoder & (step < half))
    def _():
        branch_back(False, 2 * step, *branch_args)
        feed_forward_back(False, 2 * step, *first_args)
        attention(False, 2 * step, pair_a)
        norm(False, 2 * step, pair_a)
        attention(False, 2 * step + 1, pair_b)
        norm(False, 2 * step + 1, pair_b)
        feed_forward_gradients(False, 2 * step, *weight_args)
        joint_gradient()

    @pl.when(decoder & (step == 0))
    def _():
        pl.semaphore_wait(barrier, 1 + len(others))

    @pl.when(decoder & (step < half))
    def _():
        code_copy(2 * step).start()
        code_copy(2 * step + 1).start()

    @pl.when(decoder & (step == half - 1))
    def _():
        start_reduce()

    def point(number):
        for name, turn in table[number]:
            if turn > 0:
                flows[name].advance(turn)

    @pl.when(step == half)
    def _():
        ff = acc_e.shape[1]
        rest_of = own_early[1].shape[1] - ff - width
        put_columns(own_early[1:], 0, [acc_e[...].astype(bf16), acc_m[...].astype(bf16), jnp.zeros((width, rest_of), bf16)])
        flows[1].advance(0)

    for number in range(PAIRS + 1):
        for later in range(later_steps):
            @pl.when(step == half + later)
            def _(later=later, number=number):
                point((PAIRS + 1) * later + number)

        if number < PAIRS:
            @pl.when(encoder & (step >= half))
            def _(number=number):
                attention(True, image, set_a, (number,))

    @pl.when(encoder & (step >= half))
    def _():
        norm(True, image, set_a)

    @pl.when(step == steps - 1)
    def _():
        first = own_late[0].shape[1]
        own_late[0][...] = acc_j[:, :first].astype(bf16)
        flows[2].advance(0)
        for index in range(hidden_sums.shape[1] // width):
            vectors[EXPAND_BIAS + index : EXPAND_BIAS + index + 1] = hidden_sums[:, index * width : (index + 1) * width]
        cuts = range(0, width, LANES)
        lat, rows = latent_sums[...].astype(bf16), vectors[...].astype(bf16)
        lat = jnp.concatenate([lat[:, at : at + LANES] for at in cuts], 0)
        rows = jnp.concatenate([rows[:, at : at + LANES] for at in cuts], 0)
        rows = jnp.concatenate([rows, jnp.zeros((width - rows.shape[0], LANES), bf16)], 0)
        put_columns(own_late[1:], 0, [acc_j[:, first:].astype(bf16), lat, rows, jnp.zeros((width, LANES), bf16)])
        flows[3].advance(0)
        for name, turn in rest:
            if turn > 0:
                flows[name].advance(turn)
        for flow in flows:
            flow.drain()
        for index in range(max(0, images - slots), images):
            rows_copy(index).wait()

    @pl.when((step == steps - 1) & decoder)
    def _():
        for index in range(images):
            code_copy(index).wait_send()


def finish_kernel(
    early_0, early_1, late_0, late_1, lat_columns, small_ref, rows_ref,
    wr_ref, we_ref, wj_ref, wm_ref, grad_ref, lat_ref, map_ref, be_ref, g1_ref, b1_ref, bm_ref, g2_ref, b2_ref, br_ref,
):
    width, ff = wm_ref.shape[2], we_ref.shape[2]
    early, late = (early_0, early_1), (late_0, late_1)
    grad_ref[...] = rows_ref[...].astype(f32)
    for index in range(ff // width):
        wr_ref[index] = columns(early, index * width, (index + 1) * width).astype(f32)
    we_ref[0] = columns(early, ff, 2 * ff).astype(f32)
    wm_ref[0] = columns(early, 2 * ff, 2 * ff + width).astype(f32)
    wj_ref[0] = columns(late, 0, 3 * width).astype(f32)

    @pl.when(pl.program_id(0) == 0)
    def _():
        spread = small_ref[...].astype(f32)

        def row(number):
            cuts = [spread[2 * CODE_ROWS * index + number : 2 * CODE_ROWS * index + number + 1] for index in range(width // LANES)]
            return jnp.concatenate(cuts, 1)

        tall = lat_ref.shape[1]
        for index in range(width // LANES):
            spot = lat_columns[index * tall : (index + 1) * tall]
            lat_ref[0, :, index * LANES : (index + 1) * LANES] = spot.astype(f32)
        for index in range(map_ref.shape[0]):
            map_ref[index] = row(LATENT_MAP + index)
        for piece in range(ff // width):
            be_ref[:, piece * width : (piece + 1) * width] = row(EXPAND_BIAS + piece)
        for number, ref in (
            (FIRST_GAIN, g1_ref), (FIRST_BIAS, b1_ref), (MIXER_BIAS, bm_ref), (SECOND_GAIN, g2_ref), (SECOND_BIAS, b2_ref),
            (REDUCE_BIAS, br_ref),
        ):
            ref[...] = row(number)


def whole(shape):
    return pl.BlockSpec(shape, lambda i: (0,) * len(shape), pipeline_mode=pl.Buffered(1))


def total(shape):
    return pl.BlockSpec(shape, lambda i: (0,) * len(shape))


def each(shape):
    return pl.BlockSpec((1,) + shape, lambda i: (i,) + (0,) * len(shape))


def each_second(shape):
    return pl.BlockSpec((1, 1) + shape, lambda i: (0, i) + (0,) * len(shape))


def sds(shape, dtype):
    return jax.ShapeDtypeStruct(shape, dtype)


def per_device(
    sizes, rows_in, rows_cot, counts, codes, codebook, first_gain, first_bias, joint_weight, mixer_weight, mixer_bias,
    second_gain, second_bias, expand_weight, expand_bias, reduce_weight, reduce_bias, latent_rows, latent_map,
):
    images, patch, width = rows_in.shape[1:]
    latents, code_width = latent_rows.shape[1], latent_map.shape[2]
    rows, ff = patch + latents, expand_weight.shape[2]
    entries = codebook.shape[0]
    map_cols = latent_map[0].T
    n = images
    half = n // 2
    scalars = pl.BlockSpec(memory_space=pltpu.SMEM)
    hbm = pl.BlockSpec(memory_space=pl.ANY)
    vec, wide = whole((1, width)), whole((1, ff))
    wj_spec, wm_spec = whole((1, width, 3 * width)), whole((1, width, width))
    we_spec, wr_spec = whole((1, width, ff)), whole((1, ff, width))
    saved = pl.pallas_call(
        forward_kernel,
        grid=(n,),
        in_specs=[
            scalars, each_second((patch, width)), whole((n, latents)), whole((latents, width)), whole((code_width, width)),
            whole((code_width, entries)),
            vec, vec, wj_spec, wm_spec, vec, vec, vec, we_spec, wide, wr_spec, vec,
        ],
        out_specs=[
            each_second((patch, width)), each((rows, 3 * width)), each((HEADS, rows, rows)), each((rows, width)), each((rows, width)),
            each((rows, width)), each((rows, LANES)), each((rows, width)), each((rows, ff)), each((rows, ff)),
            each((latents, width)), each((CODE_ROWS, latents)),
        ],
        out_shape=[
            sds((1, n, patch, width), bf16), sds((n, rows, 3 * width), bf16), sds((n, HEADS, rows, rows), bf16),
            sds((n, rows, width), bf16), sds((n, rows, width), bf16), sds((n, rows, width), bf16), sds((n, rows, LANES), f32),
            sds((n, rows, width), bf16), sds((n, rows, ff), bf16), sds((n, rows, ff), bf16),
            sds((n, latents, width), bf16), sds((n, CODE_ROWS, latents), f32),
        ],
        scratch_shapes=[
            pltpu.VMEM((CODE_ROWS, width), bf16), pltpu.VMEM((entries // GROUP * 3 * CODE_ROWS, GROUP), bf16),
            pltpu.VMEM((CODE_ROWS, 2 * latents), f32),
        ],
        compiler_params=pltpu.CompilerParams(vmem_limit_bytes=VMEM_BYTES),
        name="forward",
    )(
        counts, rows_in, codes, latent_rows[0], map_cols, codebook.T,
        first_gain, first_bias, joint_weight, mixer_weight, mixer_bias,
        second_gain, second_bias, expand_weight, expand_bias, reduce_weight, reduce_bias,
    )
    rows_out, joint, e, rl, mixed, x1, rs, x2, act, dg, latlow, small = saved

    def two(shape):
        return pl.BlockSpec((2,) + shape, lambda i: (jnp.minimum(i, half - 1),) + (0,) * len(shape))

    early = ahead(n)

    def first_of(shape):
        def index(i):
            mine = jnp.maximum(i - half + early, 0)
            return (jnp.where(lax.axis_index("section") == 0, mine, jnp.minimum(2 * i, n - 2)),) + (0,) * len(shape)

        return pl.BlockSpec((1,) + shape, index)

    def second_of(shape):
        def index(i):
            return (jnp.where(lax.axis_index("section") == 0, 1, jnp.minimum(2 * i + 1, n - 1)),) + (0,) * len(shape)

        return pl.BlockSpec((1,) + shape, index)

    shapes = [
        (rows, 3 * width), (HEADS, rows, rows), (rows, width), (rows, width), (rows, width), (rows, LANES), (CODE_ROWS, latents),
    ]
    shared = shapes[:4]
    pair, side, line, blocks = sizes
    ring = min(n, n - early)
    spans = (ff, ff + width + LANES, 2 * width, 2 * width)

    def flow_scratch(height, span, dtype):
        span, short = span // pair, height // side
        far = (blocks, short // line, span) if blocks > 1 else (1, 16, LANES)
        return [
            pltpu.VMEM((height, span * pair), dtype), pltpu.VMEM((height, span), dtype), pltpu.VMEM((short, span), dtype),
            pltpu.VMEM((max(1, line - 1), short // line, span), dtype), pltpu.VMEM(far, dtype),
            pltpu.VMEM((height, span * pair), dtype),
        ]

    flow_count = len(spans)
    rows_grad, *flow_sums = pl.pallas_call(
        functools.partial(backward_kernel, sizes),
        grid=(half + n - early,),
        in_specs=[
            scalars, pl.BlockSpec((1, 2, patch, width), lambda i: (0, jnp.minimum(i, half - 1), 0, 0)), two((rows, ff)),
            two((rows, ff)), two((rows, width)), two((rows, LANES)), two((rows, width)), two((latents, width)),
            two((CODE_ROWS, latents)),
            *[first_of(shape) for shape in shapes], *[second_of(shape) for shape in shared],
            whole((code_width, width)), vec, vec, wj_spec, wm_spec, vec, vec, we_spec, wr_spec,
        ],
        out_specs=[hbm] * (flow_count + 1),
        out_shape=[sds((1, n, patch, width), bf16)] + [sds((width, span), bf16) for span in spans],
        scratch_shapes=[
            pltpu.VMEM((width, ff), f32), pltpu.VMEM((width, ff), f32), pltpu.VMEM((width, 3 * width), f32),
            pltpu.VMEM((width, width), f32), pltpu.VMEM((2 * CODE_ROWS, width), f32), pltpu.VMEM((1, ff), f32),
            pltpu.VMEM((latents, width), f32),
            pltpu.VMEM((ring, rows, width), bf16), pltpu.VMEM((ring, rows, width), bf16),
            pltpu.VMEM((2 * rows, ff), bf16), pltpu.VMEM((2 * rows, width), bf16), pltpu.VMEM((2, width, 2 * rows), bf16), pltpu.VMEM((2, rows, 3 * width), bf16), pltpu.VMEM((2, width, rows), bf16),
            pltpu.VMEM((2, patch, width), bf16), pltpu.VMEM((CODE_ROWS, width), bf16),
            pltpu.VMEM((n, CODE_ROWS, latents), f32), pltpu.VMEM((n, CODE_ROWS, latents), f32),
            pltpu.SemaphoreType.DMA((n,)), pltpu.SemaphoreType.DMA((n,)), pltpu.SemaphoreType.DMA((n,)),
            pltpu.SemaphoreType.DMA((flow_count, 14)), pltpu.SemaphoreType.DMA((flow_count, 14)),
        ] + [ref for span in spans for ref in flow_scratch(width, span, bf16)],
        compiler_params=pltpu.CompilerParams(vmem_limit_bytes=VMEM_BYTES, collective_id=1, has_side_effects=True),
        name="backward",
    )(
        counts, rows_cot, act, dg, x2, rs, mixed, latlow, small,
        joint, e, rl, x1, mixed, rs, small, joint, e, rl, x1,
        map_cols, first_gain, first_bias, joint_weight, mixer_weight, second_gain, second_bias, expand_weight, reduce_weight,
    )

    parts = 4
    per = n // parts if n % parts == 0 else n
    quarter = width // parts
    vec_out, wide_out = total((1, width)), total((1, ff))

    def part(span):
        return pl.BlockSpec((quarter, span), lambda i: (i, 0))

    def out_part(height, span):
        return pl.BlockSpec((1, height, span), lambda i: (0, i, 0))

    images_part = pl.BlockSpec((1, per, patch, width), lambda i: (0, i % (n // per), 0, 0))
    wr, we, wj, wm, rows_grad, glat, gmap, gbe, g1, b1, bm, g2, b2, br = pl.pallas_call(
        finish_kernel,
        grid=(parts,),
        in_specs=[
            *[part(span) for span in spans], pl.BlockSpec((width, LANES), lambda i: (0, spans[-1] // LANES - 3)),
            pl.BlockSpec((width, LANES), lambda i: (0, spans[-1] // LANES - 2)),
            images_part,
        ],
        out_specs=[
            pl.BlockSpec((ff // width, quarter, width), lambda i: (0, i, 0)), out_part(quarter, ff), out_part(quarter, 3 * width), out_part(quarter, width),
            images_part, total((1, latents, width)), total((code_width, 1, width)), wide_out,
            vec_out, vec_out, vec_out, vec_out, vec_out, vec_out,
        ],
        out_shape=[
            sds((ff // width, width, width), f32), sds((1, width, ff), f32), sds((1, width, 3 * width), f32), sds((1, width, width), f32),
            sds((1, n, patch, width), f32), sds((1, latents, width), f32), sds((code_width, 1, width), f32), sds((1, ff), f32),
        ] + [sds((1, width), f32)] * 6,
        compiler_params=pltpu.CompilerParams(vmem_limit_bytes=VMEM_BYTES),
        name="finish",
    )(*flow_sums, flow_sums[-1], flow_sums[-1], rows_grad)
    gmap = jnp.transpose(gmap, (1, 2, 0))
    wr = wr.reshape(1, ff, width)
    return (rows_out, rows_grad, g1, b1, wj, wm, bm, g2, b2, we, gbe, wr, br, glat, gmap)


def solution(mesh):
    stacked, matrix = P("section", None), P("section", None, None)
    rows = P("section", "dp", None, None)
    placed = (
        rows, rows, P("dp"), P("dp", None), P(), stacked, stacked, matrix, matrix, stacked, stacked, stacked, matrix,
        stacked, matrix, stacked, matrix, matrix,
    )
    given = (
        rows, rows, stacked, stacked, matrix, matrix, stacked, stacked, stacked, matrix, stacked, matrix, stacked, matrix, matrix,
    )
    body = functools.partial(per_device, reach(mesh.shape["dp"]))
    return jax.shard_map(body, mesh=mesh, in_specs=placed, out_specs=given, check_vma=False)
```

time: 1170 us -> 203 us (0.17); the launches traced: 1150 us -> 203 us
  matrix products: 407 us -> 0 us
  other arithmetic: 298 us -> 0 us
  local copies, waits for them, and re-layouts: 219 us -> 0 us
  Pallas kernels: 0 us -> 202 us
  waiting for transfers between devices: 95.5 us -> 0 us
  blocking collectives: 64.6 us -> 0 us
  loops' own time: 25 us -> 0 us
  starting transfers between devices: 23.8 us -> 0 us
  between operations: 14.7 us -> 0.82 us
    dot_general x162 -> x0, matrix products: 407 us -> none  [the longest x7 104 us: block_backward(): jnp.einsum('nrd,fd->nrf', grad_branch, reduce_weight, preferred_element_t...]
    pallas_call x0 -> x3, Pallas kernels: none -> 202 us  [the longest x1 133 us: per_device(): pl.pallas_call(functools.partial(backward_kernel, sizes), grid=(half + n...]
    dynamic_update_slice x37 -> x0, other arithmetic: 116 us -> none  [the longest x30 109 us: per_device(): lax.scan(forward_step, jnp.zeros((), jnp.float32), (rows_blocks, lat_bloc...]
    psum x1 -> x0, waiting for transfers between devices: 95.5 us -> none  [per_device(): lax.psum((grads[0], grads[1], grads[2], grads[3], grads[4], grads[5], gra...]
    dynamic_slice x54 -> x0, local copies, waits for them, and re-layouts: 77 us -> none  [the longest x28 52 us: pick_block(): return lax.dynamic_index_in_dim(stacked, index, 0, keepdims=False)]
    reduce_sum x73 -> x0, other arithmetic: 64.9 us -> none  [the longest x34 40.6 us: layer_norm(): center = values - jnp.mean(values, -1, keepdims=True)]
    psum x1 -> x0, blocking collectives: 64.6 us -> none  [per_device(): lax.psum((grads[0], grads[1], grads[2], grads[3], grads[4], grads[5], gra...]
    slice x31 -> x0, local copies, waits for them, and re-layouts: 41.5 us -> none  [split_heads(): joint[:, :, start * width:(start + 1) * width]]
  transfers between devices with their start and end apart: 14 -> 0, of which waited for: 1 -> 0; matrix products, arithmetic and copies ran while one was open for 17% -> 0% of each run, Pallas kernels for 0% -> 0%
where the time goes in v1:
time: 203 us
  Pallas kernels  202 us (100%)
    pallas_call x1, Pallas kernels, per_device(): pl.pallas_call(functools.partial(backward_kernel, sizes), grid=(half + n...  133 us
    pallas_call x1, Pallas kernels, per_device(): pl.pallas_call(forward_kernel, grid=(n,), in_specs=[scalars, each_second(...  61.5 us
    pallas_call x1, Pallas kernels, per_device(): pl.pallas_call(finish_kernel, grid=(parts,), in_specs=[*[part(span) for s...  8 us

profile of v1, /device:TPU:0, one launch (start us, length us, event | category | flops | bytes accessed | tf_op | source)
XLA Modules:
  0.0 203.3 jit_solution(1690511901367424324)
XLA Ops:
  0.6 61.5 %forward.1 = (bf16[1,12,256,384]{3,2,1,0:T(8,128)(2,1)}, bf16[12,384,1152]{2,1,0:T(8,128)(2,1)}, bf16[12,6,384,384]{3,2,1,0:T(8,128)(2,1)}, bf16[12,384,384]{2,1...) custom-call(s32[12]{0:T(128)} %counts_ref.1, ...), custom_call_target="tpu_custom_call" | custom-call | tf_op jit(solution)/shard_map/forward/pallas_call | solution.py:836
  62.1 132.9 %backward.1 = (bf16[1,12,256,384]{3,2,1,0:T(8,128)(2,1)}, bf16[384,1536]{1,0:T(8,128)(2,1)}, bf16[384,2048]{1,0:T(8,128)(2,1)}, bf16[384,768]{1,0:T(8,128)(2,1)}, bf16[384,768]{1,0:T(8,128)(2,1)}) custom-call(s32[12]{0:T(128)} %counts_ref.1, bf16[1,12,256,384]{3,2,1,0:T(8,128)(2,1)} %cot_ref.1, bf16[12,384,1536]{2,1,0:T(8,128)(2,1)} %get-tuple-element.47.act_ref, ...), custom_call_target="tpu_custom_call" | custom-call | tf_op jit(solution)/shard_map/backward/pallas_call | solution.py:904
  195.1 8.0 %finish.1 = (f32[4,384,384]{2,1,0:T(8,128)}, f32[1,384,1536]{2,1,0:T(8,128)}, f32[1,384,1152]{2,1,0:T(8,128)}, f32[1,384,384]{2,1,0:T(8,128)}, f32[1,12,256,384]...) custom-call(bf16[384,1536]{1,0:T(8,128)(2,1)} %get-tuple-element.58., ...), custom_call_target="tpu_custom_call" | custom-call | tf_op jit(solution)/shard_map/finish/pallas_call | solution.py:947
